TPU v7x, 512 devices: a whole 4x4x16 slice. The times are simulated.
512 devices in a mesh: blk: 8 (over z_lo, core), grp: 64 (over x, y, z_hi).
Axes of the slice: x: 4, y: 4, z: 16 (z_hi: 4, z_lo: 4; z = z_hi * 4 + z_lo), core: 2. Of those that a mesh axis runs over, the one named last changes fastest.
Arguments:
- images: bfloat16 [131072, 1152], P(('blk', 'grp')), may hold values from -0.19921875 to 0.19921875
- texts: bfloat16 [1024, 1152], P(('blk', 'grp')), may hold values from -6 to 6
- text_proj: bfloat16 [1152, 1152], replicated, may hold values from -0.1875 to 0.1875
- labels: int32 [131072], P(('blk', 'grp')), may hold values from 0 to 1023
- logit_scale: float32 [1], replicated, may hold values from 4 to 16
- logit_bias: float32 [1], replicated, may hold values from -4 to -2
Outputs:
- image_grads: bfloat16 [131072, 1152], P(('blk', 'grp'))
- text_grads: float32 [1024, 1152], P(('blk', 'grp'))
All inputs are finite; a program needn't handle non-finite values.
Results may differ from a plain program's by a relative error of at most 0.012.
Values may be sent and summed in bfloat16 or wider, within the bound.
A program may use at most 64 MiB of HBM per device.

v0:
```python
import jax
import jax.numpy as jnp
from jax import lax
from jax.sharding import PartitionSpec as P


def passed_along(shard, axis, by):
    devices = lax.axis_size(axis)
    return lax.ppermute(shard, axis, [(i, (i + by) % devices) for i in range(devices)])


def contribute(img_emb, lab, block, text_ids, scale, bias):
    logits = (
        scale
        * lax.dot_general(
            img_emb, block, (((1,), (1,)), ((), ())), preferred_element_type=jnp.float32
        )
        + bias
    )
    sign = jnp.where(lab[:, None] == text_ids[None, :], 1.0, -1.0).astype(jnp.float32)
    dlogit = -sign * jax.nn.sigmoid(-sign * logits)
    weighted = (scale * dlogit).astype(jnp.bfloat16)
    grad_img = jnp.dot(weighted, block, preferred_element_type=jnp.float32)
    grad_txt = lax.dot_general(
        weighted, img_emb, (((0,), (0,)), ((), ())), preferred_element_type=jnp.float32
    )
    return (grad_img, grad_txt)


def local(images, texts, text_proj, labels, logit_scale, logit_bias):
    feats = images.astype(jnp.float32)
    rinv_x = lax.rsqrt(jnp.sum(feats * feats, axis=-1, keepdims=True) + 1e-06)
    unit_img = feats * rinv_x
    img_emb = unit_img.astype(jnp.bfloat16)
    proj = jnp.dot(texts, text_proj, preferred_element_type=jnp.float32)
    rinv_y = lax.rsqrt(jnp.sum(proj * proj, axis=-1, keepdims=True) + 1e-06)
    unit_txt = proj * rinv_y
    txt_emb = unit_txt.astype(jnp.bfloat16)
    scale = logit_scale[0]
    bias = logit_bias[0]
    rows_dev = texts.shape[0]
    groups = lax.axis_size("grp")
    nblocks = lax.axis_size("blk")
    here = lax.axis_index("blk")
    span = groups * rows_dev
    block_own = lax.all_gather(txt_emb, "grp", axis=0, tiled=True)
    position = jnp.arange(span, dtype=jnp.int32)
    emb_grad_img, own_acc = contribute(
        img_emb, labels, block_own, here * span + position, scale, bias
    )
    current = block_own
    travel = None
    for step in range(1, nblocks):
        current = passed_along(current, "blk", 1)
        owner = (here - step) % nblocks
        grad_img, part = contribute(img_emb, labels, current, owner * span + position, scale, bias)
        emb_grad_img = emb_grad_img + grad_img
        travel = part if travel is None else travel + part
        travel = passed_along(travel, "blk", 1)
    total = own_acc + travel
    emb_grad_txt = lax.psum_scatter(total, "grp", scatter_dimension=0, tiled=True)
    image_grads = (
        (emb_grad_img - unit_img * jnp.sum(unit_img * emb_grad_img, axis=-1, keepdims=True))
        * rinv_x
    ).astype(jnp.bfloat16)
    proj_grad = (
        (emb_grad_txt - unit_txt * jnp.sum(unit_txt * emb_grad_txt, axis=-1, keepdims=True))
        * rinv_y
    ).astype(jnp.bfloat16)
    text_grads = jnp.dot(proj_grad, text_proj.T, preferred_element_type=jnp.float32)
    return (image_grads, text_grads)


def solution(mesh):
    in_specs = (P(("blk", "grp"), None), P(("blk", "grp"), None), P(), P(("blk", "grp")), P(), P())
    out_specs = (P(("blk", "grp"), None), P(("blk", "grp"), None))
    return jax.shard_map(local, mesh=mesh, in_specs=in_specs, out_specs=out_specs, check_vma=False)
```

profile of v0, /device:TPU:6, one launch (start us, length us, event | category | flops | bytes accessed | tf_op | source)
XLA Modules:
  0.0 1137.0 jit_solution(12938981525870889898)
XLA Ops:
  10.9 208.0 %all-gather = bf16[64,2,1152]{2,1,0:T(2,128)(2,1)S(1)} all-gather(bf16[1,2,1152]{2,1,0:T(2,128)(2,1)S(1)} %fusion.82), channel_id=1, replica_groups=mesh['blk'=8,'grp'=64] {'grp'}, dimensions={0}, use_global_device_ids=true | all-gather | bytes 299520 | tf_op jit(solution)/shard_map/all_gather | solution.py:46
  219.7 1.9 collective-permute-start
  228.0 1.9 collective-permute-done
  233.1 1.9 collective-permute-start.7
  235.0 1.9 collective-permute-start.1
  240.5 9.1 collective-permute-done.1
  254.3 1.9 collective-permute-start.8
  256.3 3.3 collective-permute-done.2
  259.6 1.9 collective-permute-start.3
  262.3 5.0 collective-permute-done.8
  267.4 1.9 collective-permute-start.9
  273.2 7.2 collective-permute-done.9
  280.5 1.9 collective-permute-start.10
  283.7 1.9 collective-permute-start.5
  286.4 7.1 collective-permute-done.10
  293.5 1.9 collective-permute-start.11
  296.7 1.9 collective-permute-start.6
  299.4 7.1 collective-permute-done.11
  306.6 1.9 collective-permute-start.12
  310.5 9.1 collective-permute-done.12
  319.7 1.9 collective-permute-start.13
  323.6 9.1 collective-permute-done.13
  336.4 790.5 %all-reduce.3.cloned.1.call-done = f32[128,1152]{1,0:T(8,128)} async-done(((f32[128,1152]{1,0:T(8,128)}), f32[128,1152]{1,0:T(8,128)}) %all-reduce.3.cloned.1.call-update) | async-done | bytes 589840
  1127.9 2.2 fusion.80
  (84 shorter events, 37.8 us)
Async XLA Ops:
  7.2 214.5 %copy-start.1 = (bf16[256,1152]{1,0:T(8,128)(2,1)S(1)}, bf16[256,1152]{1,0:T(8,128)(2,1)}, u32[]{:S(2)}) copy-start(bf16[256,1152]{1,0:T(8,128)(2,1)} %param.6) | copy-start | bytes 1769476
  7.2 1119.8 %all-reduce.3.cloned.1.call-start = ((), (), s32[]{:S(2)}) async-start(), calls=%async_computation | async-start | bytes 1179648
  219.7 10.1 collective-permute-start
  229.9 9.4 copy-start.3
  233.1 19.8 %collective-permute-start.7 = (f32[128,1152]{1,0:T(8,128)}, f32[128,1152]{1,0:T(8,128)}, u32[]{:S(2)}, u32[]{:S(2)}) collective-permute-start(f32[128,1152]{1,0:T(8,128)} %fusion.95), channel_id=1, source_target_pairs={{0,64},{64,128},{128,192},{192,256},{256,320},{320,384},{384,448},... | collective-permute-start | bytes 1769480 | tf_op jit(solution)/shard_map/ppermute | solution.py:9
  235.0 14.5 %collective-permute-start.1 = (bf16[128,1152]{1,0:T(8,128)(2,1)}, bf16[128,1152]{1,0:T(8,128)(2,1)}, u32[]{:S(2)}, u32[]{:S(2)}) collective-permute-start(bf16[128,1152]{1,0:T(8,128)(2,1)} %collective-permute-done), channel_id=1, source_target_pairs={{0,64},{64,128},{128,192},{192,256},{256,320},{320,384},{384,448},... | collective-permute-start | bytes 884744 | tf_op jit(solution)/shard_map/ppermute | solution.py:9
  249.6 10.0 collective-permute-start.2
  252.9 8.6 copy-start.10
  252.9 8.6 copy-start.12
  254.3 13.0 %collective-permute-start.8 = (f32[128,1152]{1,0:T(8,128)S(1)}, f32[128,1152]{1,0:T(8,128)S(1)}, u32[]{:S(2)}, u32[]{:S(2)}) collective-permute-start(f32[128,1152]{1,0:T(8,128)S(1)} %convolution_add_fusion.7), channel_id=1, source_target_pairs={{0,64},{64,128},{128,192},{192,256},{256,320},{320,384},{384,448},... | collective-permute-start | bytes 1769480 | tf_op jit(solution)/shard_map/ppermute | solution.py:9
  259.6 10.9 collective-permute-start.3
  262.3 10.1 copy-start.11
  267.4 13.0 %collective-permute-start.9 = (f32[128,1152]{1,0:T(8,128)S(1)}, f32[128,1152]{1,0:T(8,128)S(1)}, u32[]{:S(2)}, u32[]{:S(2)}) collective-permute-start(f32[128,1152]{1,0:T(8,128)S(1)} %add.281), channel_id=1, source_target_pairs={{0,64},{64,128},{128,192},{192,256},{256,320},{320,384},{384,448},... | collective-permute-start | bytes 1769480 | tf_op jit(solution)/shard_map/ppermute | solution.py:9
  270.5 13.2 %collective-permute-start.4 = (bf16[128,1152]{1,0:T(8,128)(2,1)S(1)}, bf16[128,1152]{1,0:T(8,128)(2,1)S(1)}, u32[]{:S(2)}, u32[]{:S(2)}) collective-permute-start(bf16[128,1152]{1,0:T(8,128)(2,1)S(1)} %collective-permute-done.3), channel_id=1, source_target_pairs={{0,64},{64,128},{128,192},{192,256},{256,320},{320,384},{384,448},... | collective-permute-start | bytes 884744 | tf_op jit(solution)/shard_map/ppermute | solution.py:9
  273.2 9.2 copy-start.5
  280.5 13.0 %collective-permute-start.10 = (f32[128,1152]{1,0:T(8,128)S(1)}, f32[128,1152]{1,0:T(8,128)S(1)}, u32[]{:S(2)}, u32[]{:S(2)}) collective-permute-start(f32[128,1152]{1,0:T(8,128)S(1)} %add.282), channel_id=1, source_target_pairs={{0,64},{64,128},{128,192},{192,256},{256,320},{320,384},{384,448},... | collective-permute-start | bytes 1769480 | tf_op jit(solution)/shard_map/ppermute | solution.py:9
  283.7 13.0 %collective-permute-start.5 = (bf16[128,1152]{1,0:T(8,128)(2,1)S(1)}, bf16[128,1152]{1,0:T(8,128)(2,1)S(1)}, u32[]{:S(2)}, u32[]{:S(2)}) collective-permute-start(bf16[128,1152]{1,0:T(8,128)(2,1)S(1)} %collective-permute-done.4), channel_id=1, source_target_pairs={{0,64},{64,128},{128,192},{192,256},{256,320},{320,384},{384,448},... | collective-permute-start | bytes 884744 | tf_op jit(solution)/shard_map/ppermute | solution.py:9
  293.5 13.0 %collective-permute-start.11 = (f32[128,1152]{1,0:T(8,128)S(1)}, f32[128,1152]{1,0:T(8,128)S(1)}, u32[]{:S(2)}, u32[]{:S(2)}) collective-permute-start(f32[128,1152]{1,0:T(8,128)S(1)} %add.283), channel_id=1, source_target_pairs={{0,64},{64,128},{128,192},{192,256},{256,320},{320,384},{384,448},... | collective-permute-start | bytes 1769480 | tf_op jit(solution)/shard_map/ppermute | solution.py:9
  296.7 13.0 %collective-permute-start.6 = (bf16[128,1152]{1,0:T(8,128)(2,1)S(1)}, bf16[128,1152]{1,0:T(8,128)(2,1)S(1)}, u32[]{:S(2)}, u32[]{:S(2)}) collective-permute-start(bf16[128,1152]{1,0:T(8,128)(2,1)S(1)} %collective-permute-done.5), channel_id=1, source_target_pairs={{0,64},{64,128},{128,192},{192,256},{256,320},{320,384},{384,448},... | collective-permute-start | bytes 884744 | tf_op jit(solution)/shard_map/ppermute | solution.py:9
  306.6 13.0 %collective-permute-start.12 = (f32[128,1152]{1,0:T(8,128)S(1)}, f32[128,1152]{1,0:T(8,128)S(1)}, u32[]{:S(2)}, u32[]{:S(2)}) collective-permute-start(f32[128,1152]{1,0:T(8,128)S(1)} %add.284), channel_id=1, source_target_pairs={{0,64},{64,128},{128,192},{192,256},{256,320},{320,384},{384,448},... | collective-permute-start | bytes 1769480 | tf_op jit(solution)/shard_map/ppermute | solution.py:9
  310.1 9.6 copy-start.7
  319.7 13.0 %collective-permute-start.13 = (f32[128,1152]{1,0:T(8,128)S(1)}, f32[128,1152]{1,0:T(8,128)S(1)}, u32[]{:S(2)}, u32[]{:S(2)}) collective-permute-start(f32[128,1152]{1,0:T(8,128)S(1)} %add.285), channel_id=1, source_target_pairs={{0,64},{64,128},{128,192},{192,256},{256,320},{320,384},{384,448},... | collective-permute-start | bytes 1769480 | tf_op jit(solution)/shard_map/ppermute | solution.py:9
  322.2 10.5 copy-start.2
  335.3 791.7 %copy-start.9 = (f32[2]{0:T(128)S(1)}, f32[2]{0:T(128)}, u32[]{:S(2)}) copy-start(f32[2]{0:T(128)} %copy-done.8) | copy-start | bytes 28
  (5 other events, 11.8 us)
Sparse Core Ops, SparseCore 0:
  333.7 793.2 all-reduce.2
where the time goes:
time: 1160 us; the launch traced here: 1140 us
  waiting for transfers between devices  851 us (73%)
  blocking collectives  208 us (18%)
  starting transfers between devices  26.9 us (2%)
  matrix products  22.8 us (2%)
  between operations  16.5 us (1%)
    unnamed x2, waiting for transfers between devices  791 us
    all_gather x1, blocking collectives, local(): block_own = lax.all_gather(txt_emb, 'grp', axis=0, tiled=True)  208 us
    ppermute x14, waiting for transfers between devices, passed_along(): lax.ppermute(shard, axis, [(i, (i + by) % devices) for i in range(devices)])  60.9 us
    ppermute x14, starting transfers between devices, passed_along(): lax.ppermute(shard, axis, [(i, (i + by) % devices) for i in range(devices)])  26.8 us
  transfers between devices with their start and end apart: 15, of which 12 were waited for; matrix products, arithmetic and copies ran while one was open for 2% of the time, Pallas kernels for 0%

commit v1 on v0

v1 whole, which is shorter than its diff:
```python
import functools

import jax
import jax.numpy as jnp
from jax import lax
from jax.experimental import pallas as pl
from jax.experimental.pallas import tpu as pltpu
from jax.sharding import PartitionSpec as P

MESH = pl.DeviceIdType.MESH
BF = jnp.bfloat16
F32 = jnp.float32
D = 1152
NI = 256
EPS = 1e-06
NT = (((1,), (1,)), ((), ()))
TN = (((0,), (0,)), ((), ()))


def mod(a, n):
    return lax.rem(a + n, n)


def device(x, y, z, c):
    return {
        "blk": lax.rem(z, 4) * 2 + c,
        "grp": x * 16 + y * 4 + lax.div(z, 4),
    }


def sigmoid_grad(logits, match, scale):
    t = jnp.where(match, -logits, logits)
    s = scale / (1.0 + jnp.exp(-t))
    return jnp.where(match, -s, s).astype(BF)


def kernel(
    images, texts, proj_w, labels, scale_ref, bias_ref,
    out_img, out_txt,
    imgs, emb, wv, lab2, zin, ta, tb, e_txt, wt, proj_own, gtx, gimg_out, gimg_in, outv,
    s1a, s1b, r1a, r1b, acc_a, acc_b, s2a, s2b, r2a, r2b, fa, fb, zout, zr,
    sem_local, sem_core_s, sem_core_r, sem_z_s, sem_z_r, sem_s_s, sem_s_r,
    sem_b_s, sem_b_r, sem_r1_s, sem_r1_r, sem_r2_s, sem_r2_r, sem_r3_s, sem_r3_r,
):
    blk = lax.axis_index("blk")
    grp = lax.axis_index("grp")
    c = lax.rem(blk, 2)
    z = lax.rem(grp, 4) * 4 + lax.div(blk, 2)
    x = lax.div(grp, 16)
    y = lax.rem(lax.div(grp, 4), 4)

    def remote(src, dst, ss, rs, dx=0, dy=0, dz=0, dc=0):
        return pltpu.make_async_remote_copy(
            src_ref=src, dst_ref=dst, send_sem=ss, recv_sem=rs,
            device_id=device(mod(x + dx, 4), mod(y + dy, 4), mod(z + dz, 16), mod(c + dc, 2)),
            device_id_type=MESH,
        )

    load_img = pltpu.make_async_copy(images, imgs.at[0], sem_local.at[0])
    load_w = pltpu.make_async_copy(proj_w, wv, sem_local.at[1])
    load_img.start()
    load_w.start()

    barrier = pltpu.get_barrier_semaphore()
    partners = [dict(dc=1)] + [dict(dx=d) for d in (1, 2, 3)] + [dict(dy=d) for d in (1, 2, 3)]
    partners += [dict(dz=d) for d in range(1, 16)]
    for p in partners:
        who = device(mod(x + p.get("dx", 0), 4), mod(y + p.get("dy", 0), 4),
                     mod(z + p.get("dz", 0), 16), mod(c + p.get("dc", 0), 2))
        pl.semaphore_signal(barrier, inc=1, device_id=who, device_id_type=MESH)
    pl.semaphore_wait(barrier, len(partners))

    zs = [remote(texts, zin.at[z], sem_z_s.at[d], sem_z_r.at[d], dz=d) for d in range(1, 16)]
    for cp in zs:
        cp.start()
    core_img = remote(images, imgs.at[1], sem_core_s.at[0], sem_core_r.at[0], dc=1)
    core_lab = remote(labels, lab2.at[1], sem_core_s.at[1], sem_core_r.at[1], dc=1)
    core_lab.start()
    core_img.start()
    zin[z] = texts[...]
    lab2[0] = labels[...]

    load_w.wait()
    proj_own[...] = jnp.dot(texts[...], wv[...], preferred_element_type=F32)

    def embed(half):
        def step(i, carry):
            rows = pl.ds(pl.multiple_of(i * 64, 64), 64)
            f = imgs[half, rows, :].astype(F32)
            r = lax.rsqrt(jnp.sum(f * f, axis=-1, keepdims=True) + EPS)
            emb[pl.ds(pl.multiple_of(half * NI + i * 64, 64), 64), :] = (f * r).astype(BF)
            return carry
        lax.fori_loop(0, NI // 64, step, 0)

    load_img.wait()
    embed(0)
    core_img.wait()
    core_lab.wait()
    embed(1)

    for cp in zs:
        cp.wait()
    zall = zin[...].astype(F32)
    ta[y, x] = zall[:, 0, :].astype(BF)
    tb[x, y] = zall[:, 1, :].astype(BF)

    small_a = [remote(ta.at[y, x], ta.at[y, x], sem_s_s.at[0, d], sem_s_r.at[0, d], dx=d) for d in (1, 2, 3)]
    small_b = [remote(tb.at[x, y], tb.at[x, y], sem_s_s.at[1, d], sem_s_r.at[1, d], dy=d) for d in (1, 2, 3)]
    for a, b in zip(small_a, small_b):
        a.start()
        b.start()
    bulk = []

    def forward(e):
        xs, ys = mod(x - e, 4), mod(y - e, 4)
        for d in (1, 3, 2):
            a = remote(ta.at[y, xs], ta.at[y, xs], sem_b_s.at[0, e, d], sem_b_r.at[0, e, d], dy=d)
            b = remote(tb.at[x, ys], tb.at[x, ys], sem_b_s.at[1, e, d], sem_b_r.at[1, e, d], dx=d)
            a.start()
            b.start()
            bulk.append(a)
            bulk.append(b)

    forward(0)
    for e in (1, 3, 2):
        small_a[e - 1].wait_recv()
        small_b[e - 1].wait_recv()
        forward(e)
    for cp in small_a + small_b:
        cp.wait_send()
    for cp in bulk:
        cp.wait()

    def project(i, carry):
        h = lax.div(i, 2)
        for part, t in ((0, ta), (1, tb)):
            @pl.when(h == part)
            def _():
                k = lax.rem(i, 2) * 2
                rows = t[pl.ds(k, 2)].reshape(128, D)
                p = jnp.dot(rows, wv[...], preferred_element_type=F32)
                r = lax.rsqrt(jnp.sum(p * p, axis=-1, keepdims=True) + EPS)
                e_txt[pl.ds(pl.multiple_of(i * 128, 128), 128), :] = (p * r).astype(BF)
        return carry

    lax.fori_loop(0, 4, project, 0)

    scale = scale_ref[0]
    bias = bias_ref[0]

    lab = jnp.concatenate([lab2[0][None, :], lab2[1][None, :]], axis=1)
    lr = lab & 1
    lz = ((lab >> 1) & 3) * 4 + ((lab >> 8) & 3)
    ly = (lab >> 3) & 3
    lx = (lab >> 5) & 3
    lc = (lab >> 7) & 1
    pos = jnp.where(lr == 0, (ly * 4 + lx) * 16 + lz, 256 + (lx * 4 + ly) * 16 + lz)
    pos = jnp.where(lc == c, pos, -1)

    def weigh(i, carry):
        rows = pl.ds(pl.multiple_of(i * 128, 128), 128)
        logits = lax.dot_general(e_txt[rows, :], emb[...], NT, preferred_element_type=F32)
        logits = scale * logits + bias
        ids = lax.broadcasted_iota(jnp.int32, logits.shape, 0) + i * 128
        w = sigmoid_grad(logits, ids == pos, scale)
        wt[rows, :] = w
        g = jnp.dot(w, emb[...], preferred_element_type=F32)
        gtx[rows, :] = g
        return carry

    lax.fori_loop(0, 4, weigh, 0)

    r1 = []
    for d in (2, 1, 3):
        yy, xx = mod(y + d, 4), mod(x + d, 4)
        s1a[d - 1] = gtx[pl.ds(pl.multiple_of(yy * 64, 64), 64), :].astype(BF)
        s1b[d - 1] = gtx[pl.ds(pl.multiple_of(256 + xx * 64, 64), 64), :].astype(BF)
        a = remote(s1a.at[d - 1], r1a.at[d - 1], sem_r1_s.at[0, d], sem_r1_r.at[0, d], dy=d)
        b = remote(s1b.at[d - 1], r1b.at[d - 1], sem_r1_s.at[1, d], sem_r1_r.at[1, d], dx=d)
        a.start()
        b.start()
        r1 += [a, b]

    def image_part(half):
        def step(i, carry):
            cols = pl.ds(pl.multiple_of(half * NI + i * 128, 128), 128)
            g = lax.dot_general(wt[:, cols], e_txt[...], TN, preferred_element_type=F32)
            rows = pl.ds(pl.multiple_of(i * 128, 128), 128)
            if half == 1:
                gimg_out[rows, :] = g.astype(BF)
            else:
                outv[rows, :] = g
            return carry
        lax.fori_loop(0, 2, step, 0)

    image_part(1)
    core_grad = remote(gimg_out, gimg_in, sem_core_s.at[2], sem_core_r.at[2], dc=1)
    core_grad.start()
    image_part(0)

    for cp in r1:
        cp.wait()
    own = gtx[pl.ds(pl.multiple_of(y * 64, 64), 64), :]
    acc_a[...] = own + r1a[0].astype(F32) + r1a[1].astype(F32) + r1a[2].astype(F32)
    own = gtx[pl.ds(pl.multiple_of(256 + x * 64, 64), 64), :]
    acc_b[...] = own + r1b[0].astype(F32) + r1b[1].astype(F32) + r1b[2].astype(F32)
    r2 = []
    for d in (2, 1, 3):
        xx, yy = mod(x + d, 4), mod(y + d, 4)
        s2a[d - 1] = acc_a[pl.ds(pl.multiple_of(xx * 16, 16), 16), :].astype(BF)
        s2b[d - 1] = acc_b[pl.ds(pl.multiple_of(yy * 16, 16), 16), :].astype(BF)
        a = remote(s2a.at[d - 1], r2a.at[d - 1], sem_r2_s.at[0, d], sem_r2_r.at[0, d], dx=d)
        b = remote(s2b.at[d - 1], r2b.at[d - 1], sem_r2_s.at[1, d], sem_r2_r.at[1, d], dy=d)
        a.start()
        b.start()
        r2 += [a, b]
    for cp in r2:
        cp.wait()
    own = acc_a[pl.ds(pl.multiple_of(x * 16, 16), 16), :]
    sum_a = own + r2a[0].astype(F32) + r2a[1].astype(F32) + r2a[2].astype(F32)
    own = acc_b[pl.ds(pl.multiple_of(y * 16, 16), 16), :]
    sum_b = own + r2b[0].astype(F32) + r2b[1].astype(F32) + r2b[2].astype(F32)
    fa[...] = sum_a
    fb[...] = sum_b
    for k in range(16):
        zout[k] = jnp.concatenate([sum_a[k : k + 1, :], sum_b[k : k + 1, :]], axis=0).astype(BF)
    r3 = []
    for d in (8, 7, 9, 6, 10, 5, 11, 4, 12, 3, 13, 2, 14, 1, 15):
        cp = remote(zout.at[mod(z + d, 16)], zr.at[d], sem_r3_s.at[d], sem_r3_r.at[d], dz=d)
        cp.start()
        r3.append(cp)

    core_grad.wait()

    def finish(i, carry):
        rows = pl.ds(pl.multiple_of(i * 64, 64), 64)
        g = outv[rows, :] + gimg_in[rows, :].astype(F32)
        f = imgs[0, rows, :].astype(F32)
        r = lax.rsqrt(jnp.sum(f * f, axis=-1, keepdims=True) + EPS)
        u = f * r
        g = (g - u * jnp.sum(u * g, axis=-1, keepdims=True)) * r
        gimg_out[rows, :] = g.astype(BF)
        return carry

    lax.fori_loop(0, NI // 64, finish, 0)
    store = pltpu.make_async_copy(gimg_out, out_img, sem_local.at[2])
    store.start()

    for cp in r3:
        cp.wait()
    total = jnp.concatenate([fa[pl.ds(z, 1), :], fb[pl.ds(z, 1), :]], axis=0)
    for d in range(1, 16):
        total = total + zr[d].astype(F32)
    p = proj_own[...]
    r = lax.rsqrt(jnp.sum(p * p, axis=-1, keepdims=True) + EPS)
    u = p * r
    pg = ((total - u * jnp.sum(u * total, axis=-1, keepdims=True)) * r).astype(BF)
    out_txt[...] = lax.dot_general(pg, wv[...], NT, preferred_element_type=F32)
    store.wait()


def local(images, texts, text_proj, labels, logit_scale, logit_bias):
    vmem = pl.BlockSpec(memory_space=pltpu.VMEM)
    smem = pl.BlockSpec(memory_space=pltpu.SMEM)
    hbm = pl.BlockSpec(memory_space=pl.ANY)
    dma = pltpu.SemaphoreType.DMA
    scratch = [
        pltpu.VMEM((2, NI, D), BF),
        pltpu.VMEM((2 * NI, D), BF),
        pltpu.VMEM((D, D), BF),
        pltpu.VMEM((2, NI), jnp.int32),
        pltpu.VMEM((16, 2, D), BF),
        pltpu.VMEM((4, 4, 16, D), BF),
        pltpu.VMEM((4, 4, 16, D), BF),
        pltpu.VMEM((512, D), BF),
        pltpu.VMEM((512, 2 * NI), BF),
        pltpu.VMEM((2, D), F32),
        pltpu.VMEM((512, D), F32),
        pltpu.VMEM((NI, D), BF),
        pltpu.VMEM((NI, D), BF),
        pltpu.VMEM((NI, D), F32),
        pltpu.VMEM((3, 64, D), BF),
        pltpu.VMEM((3, 64, D), BF),
        pltpu.VMEM((3, 64, D), BF),
        pltpu.VMEM((3, 64, D), BF),
        pltpu.VMEM((64, D), F32),
        pltpu.VMEM((64, D), F32),
        pltpu.VMEM((3, 16, D), BF),
        pltpu.VMEM((3, 16, D), BF),
        pltpu.VMEM((3, 16, D), BF),
        pltpu.VMEM((3, 16, D), BF),
        pltpu.VMEM((16, D), F32),
        pltpu.VMEM((16, D), F32),
        pltpu.VMEM((16, 2, D), BF),
        pltpu.VMEM((16, 2, D), BF),
        dma((3,)), dma((3,)), dma((3,)), dma((16,)), dma((16,)), dma((2, 4)), dma((2, 4)),
        dma((2, 4, 4)), dma((2, 4, 4)), dma((2, 4)), dma((2, 4)), dma((2, 4)), dma((2, 4)),
        dma((16,)), dma((16,)),
    ]
    return pl.pallas_call(
        kernel,
        out_shape=(
            jax.ShapeDtypeStruct((NI, D), BF),
            jax.ShapeDtypeStruct((2, D), F32),
        ),
        in_specs=[hbm, vmem, hbm, vmem, smem, smem],
        out_specs=(hbm, vmem),
        scratch_shapes=scratch,
        compiler_params=pltpu.CompilerParams(
            collective_id=0, has_side_effects=True, vmem_limit_bytes=50 * 2**20
        ),
        cost_estimate=pl.CostEstimate(flops=4 * 10**9, bytes_accessed=8 * 10**6, transcendentals=10**6),
        name="reward_backward",
    )(images, texts, text_proj, labels, logit_scale, logit_bias)


def solution(mesh):
    in_specs = (P(("blk", "grp"), None), P(("blk", "grp"), None), P(), P(("blk", "grp")), P(), P())
    out_specs = (P(("blk", "grp"), None), P(("blk", "grp"), None))
    return jax.shard_map(local, mesh=mesh, in_specs=in_specs, out_specs=out_specs, check_vma=False)
```

time: 1160 us -> 71.1 us (0.06); the launches traced: 1140 us -> 70.8 us
  waiting for transfers between devices: 851 us -> 0 us
  blocking collectives: 208 us -> 0 us
  Pallas kernels: 0 us -> 63.3 us
  starting transfers between devices: 26.9 us -> 0 us
  matrix products: 22.8 us -> 0 us
  between operations: 16.5 us -> 1.94 us
    unnamed x2 -> x0, waiting for transfers between devices: 791 us -> none
    all_gather x1 -> x0, blocking collectives: 208 us -> none  [local(): block_own = lax.all_gather(txt_emb, 'grp', axis=0, tiled=True)]
    pallas_call x0 -> x1, Pallas kernels: none -> 63.3 us  [local(): pl.pallas_call(kernel, out_shape=(jax.ShapeDtypeStruct((NI, D), BF), jax....]
    ppermute x14 -> x0, waiting for transfers between devices: 60.9 us -> none  [passed_along(): lax.ppermute(shard, axis, [(i, (i + by) % devices) for i in range(devices)])]
    ppermute x14 -> x0, starting transfers between devices: 26.8 us -> none  [passed_along(): lax.ppermute(shard, axis, [(i, (i + by) % devices) for i in range(devices)])]
    dot_general x26 -> x0, matrix products: 22.8 us -> none  [the longest x8 7.68 us: contribute(): grad_img = jnp.dot(weighted, block, preferred_element_type=jnp.float32)]
  transfers between devices with their start and end apart: 15 -> 0, of which waited for: 12 -> 0; matrix products, arithmetic and copies ran while one was open for 2% -> 0% of each run, Pallas kernels for 0% -> 0%
where the time goes in v1:
time: 71.1 us; the launch traced here: 70.8 us
  Pallas kernels  63.3 us (89%)
  local copies, waits for them, and re-layouts  5.59 us (8%)
  between operations  1.94 us (3%)
    pallas_call x1, Pallas kernels, local(): pl.pallas_call(kernel, out_shape=(jax.ShapeDtypeStruct((NI, D), BF), jax....  63.3 us
    unnamed x10, local copies, waits for them, and re-layouts  5.59 us

profile of v1, /device:TPU:6, one launch (start us, length us, event | category | flops | bytes accessed | tf_op | source)
XLA Modules:
  0.0 70.8 jit_solution(13011266991742947035)
XLA Ops:
  1.9 0.0 copy-start
  1.9 1.7 %copy-done = bf16[1152,1152]{1,0:T(8,128)(2,1)S(1)} copy-done((bf16[1152,1152]{1,0:T(8,128)(2,1)S(1)}, bf16[1152,1152]{1,0:T(8,128)(2,1)}, u32[]{:S(2)}) %copy-start) | copy-done | bytes 2654232
  3.7 0.0 copy-start.1
  3.7 1.1 %copy-done.1 = bf16[256,1152]{1,0:T(8,128)(2,1)S(1)} copy-done((bf16[256,1152]{1,0:T(8,128)(2,1)S(1)}, bf16[256,1152]{1,0:T(8,128)(2,1)}, u32[]{:S(2)}) %copy-start.1) | copy-done | bytes 589848
  4.7 0.0 copy-start.2
  4.7 0.7 copy-done.2
  5.4 0.0 copy-start.3
  5.4 0.7 copy-done.3
  6.1 63.3 %reward_backward.1 = (bf16[256,1152]{1,0:T(8,128)(2,1)S(1)}, f32[2,1152]{1,0:T(2,128)S(1)}) custom-call(bf16[256,1152]{1,0:T(8,128)(2,1)S(1)} %copy-done.1, bf16[2,1152]{1,0:T(2,128)(2,1)S(1)} %copy-done.2, bf16[1152,1152]{1,0:T(8,128)(2,1)S(1)} %copy-done, s32[256]{0:T(256)S(1)} %copy-done.3, f32[1]{0:T(128)S(6)} %copy.10.scale_ref, f32[1]{0:T(128)S(6)} %copy.11.bias_ref), custom_call_target="tpu_custom_call" | custom-call | flops 4000000000 | bytes 8000000 | tf_op jit(solution)/shard_map/reward_backward/pallas_call | solution.py:300
  69.4 0.8 %copy.12 = bf16[256,1152]{1,0:T(8,128)(2,1)} copy(bf16[256,1152]{1,0:T(8,128)(2,1)S(1)} %get-tuple-element.4) | data formatting | bytes 1179648
  70.2 0.6 copy.13
Async XLA Ops:
  1.9 1.8 %copy-start = (bf16[1152,1152]{1,0:T(8,128)(2,1)S(1)}, bf16[1152,1152]{1,0:T(8,128)(2,1)}, u32[]{:S(2)}) copy-start(bf16[1152,1152]{1,0:T(8,128)(2,1)} %proj_w.1) | copy-start | bytes 7962628
  3.7 1.1 %copy-start.1 = (bf16[256,1152]{1,0:T(8,128)(2,1)S(1)}, bf16[256,1152]{1,0:T(8,128)(2,1)}, u32[]{:S(2)}) copy-start(bf16[256,1152]{1,0:T(8,128)(2,1)} %images.1) | copy-start | bytes 1769476
  4.7 0.7 copy-start.2
  5.4 0.7 copy-start.3

commit v2 on v0

v2 whole, which is shorter than its diff:
```python
import jax
import jax.numpy as jnp
from jax import lax
from jax.experimental import pallas as pl
from jax.experimental.pallas import tpu as pltpu
from jax.sharding import PartitionSpec as P

MESH = pl.DeviceIdType.MESH
BF = jnp.bfloat16
F32 = jnp.float32
D = 1152
NI = 256
EPS = 1e-06
NT = (((1,), (1,)), ((), ()))
TN = (((0,), (0,)), ((), ()))
STEPS = (0, -1, -2, -3, 1, 2, 3, 4, 5, 6, 7, 8, -4, -5, -6, -7)
NEAR = (7, 6, 3, 5, 2, 4, 1)
SEG = 128


def mod(a, n):
    return lax.rem(a + n, n)


def unit(v):
    r = lax.rsqrt(jnp.sum(v * v, axis=-1, keepdims=True) + EPS)
    return v * r, r


def kernel(
    images, texts, proj_w, labels, scale_ref, bias_ref,
    out_img, out_txt,
    scal, imgs, emb, wv, lab_a, lab_b, zin, tx, e_txt, wt, proj_own, gimg_out, gimg_in, gimg,
    own1, s1, r1, own2, s2, r2, own3, zout, zr,
    sem_l, sem_cs, sem_cr, sem_zs, sem_zr, sem_ss, sem_sr, sem_bs, sem_br,
    sem_1s, sem_1r, sem_2s, sem_2r, sem_3s, sem_3r,
):
    blk = lax.axis_index("blk")
    grp = lax.axis_index("grp")
    c = lax.rem(blk, 2)
    z = lax.rem(grp, 4) * 4 + lax.div(blk, 2)
    x = lax.div(grp, 16)
    y = lax.rem(lax.div(grp, 4), 4)

    def device(dx=0, dy=0, dz=0, dc=0):
        tz = mod(z + dz, 16)
        return {
            "blk": lax.rem(tz, 4) * 2 + mod(c + dc, 2),
            "grp": mod(x + dx, 4) * 16 + mod(y + dy, 4) * 4 + lax.div(tz, 4),
        }

    def remote(src, dst, ss, rs, **to):
        return pltpu.make_async_remote_copy(
            src_ref=src, dst_ref=dst, send_sem=ss, recv_sem=rs,
            device_id=device(**to), device_id_type=MESH,
        )

    def along(half, by, first):
        return {"dx" if (half == 0) == first else "dy": by}

    loads = [
        pltpu.make_async_copy(texts, zin.at[0], sem_l.at[0]),
        pltpu.make_async_copy(labels, lab_a, sem_l.at[1]),
        pltpu.make_async_copy(images, imgs.at[0], sem_l.at[2]),
        pltpu.make_async_copy(proj_w, wv, sem_l.at[3]),
        pltpu.make_async_copy(scale_ref, scal.at[0], sem_l.at[5]),
        pltpu.make_async_copy(bias_ref, scal.at[1], sem_l.at[6]),
    ]
    for cp in loads:
        cp.start()

    barrier = pltpu.get_barrier_semaphore()
    partners = [dict(dz=d) for d in (4, -4, 3, -3, 2, -2, 1, -1)]
    partners += [dict(dx=d) for d in (1, 2, 3)] + [dict(dy=d) for d in (1, 2, 3)] + [dict(dc=1)]
    for p in partners:
        pl.semaphore_signal(barrier, inc=1, device_id=device(**p), device_id_type=MESH)
    for cp in loads:
        cp.wait()
    pl.semaphore_wait(barrier, len(partners))

    zs = {}
    for k in NEAR:
        zs[k] = remote(zin.at[0], zin.at[k], sem_zs.at[k], sem_zr.at[k], dz=STEPS[k])
        zs[k].start()
    core_lab = remote(lab_a, lab_b, sem_cs.at[0], sem_cr.at[0], dc=1)
    core_img = remote(imgs.at[0], imgs.at[1], sem_cs.at[1], sem_cr.at[1], dc=1)
    core_lab.start()
    core_img.start()

    proj_own[...] = jnp.dot(zin[0], wv[...], preferred_element_type=F32)

    def embed(half):
        def step(i, carry):
            u, _ = unit(imgs[half, pl.ds(pl.multiple_of(i * 64, 64), 64), :].astype(F32))
            emb[pl.ds(pl.multiple_of(half * NI + i * 64, 64), 64), :] = u.astype(BF)
            return carry
        lax.fori_loop(0, NI // 64, step, 0)

    embed(0)

    def small(s):
        copies = []
        for d in (2, 1, 3):
            cp = remote(tx.at[s, 0, 0], tx.at[s, 0, d], sem_ss.at[s, d], sem_sr.at[s, d], **along(s % 2, d, True))
            cp.start()
            copies.append(cp)
        return copies

    def spread(s, arriving):
        for cp in arriving:
            cp.wait_recv()
        copies = []
        for d in (2, 1, 3):
            cp = remote(tx.at[s, 0], tx.at[s, d], sem_bs.at[s, d], sem_br.at[s, d], **along(s % 2, d, False))
            cp.start()
            copies.append(cp)
        return copies

    def place(s):
        for k in range(4 * s, 4 * s + 4):
            if k:
                zs[k].wait_recv()
        tx[s, 0, 0] = zin[4 * s : 4 * s + 4].astype(F32).reshape(8, D).astype(BF)
        on = remote(tx.at[s, 0, 0], tx.at[3 - s, 0, 0], sem_zs.at[8 + s], sem_zr.at[8 + s], dz=(-4, 4)[s])
        on.start()
        return on

    on0 = place(0)
    small0 = small(0)
    on1 = place(1)
    small1 = small(1)
    bulk0 = spread(0, small0)
    bulk1 = spread(1, small1)
    core_lab.wait()
    core_img.wait()
    embed(1)
    on0.wait_recv()
    small3 = small(3)
    on1.wait_recv()
    small2 = small(2)
    bulk3 = spread(3, small3)
    bulk2 = spread(2, small2)

    scale = scal[0, 0, 0]
    bias = scal[1, 0, 0]

    lab = jnp.concatenate([lab_a[...][None, :], lab_b[...][None, :]], axis=1)
    ez = mod(z - (((lab >> 1) & 3) * 4 + ((lab >> 8) & 3)), 16)
    ey = mod(y - ((lab >> 3) & 3), 4)
    ex = mod(x - ((lab >> 5) & 3), 4)
    kz = jnp.where(ez == 0, 0, jnp.where(ez <= 8, ez + 3, jnp.where(ez >= 13, 16 - ez, 24 - ez)))
    seg = kz >> 2
    first_axis = (seg & 1) == 0
    i2 = jnp.where(first_axis, ey, ex)
    i1 = jnp.where(first_axis, ex, ey)
    pos = seg * SEG + i2 * 32 + i1 * 8 + (kz & 3) * 2 + (lab & 1)
    pos = jnp.where(((lab >> 7) & 1) == c, pos, -1)

    def segment(s, copies):
        half = s % 2
        for cp in copies:
            cp.wait_recv()
        rows = pl.ds(s * SEG, SEG)
        p = jnp.dot(tx[s].reshape(SEG, D), wv[...], preferred_element_type=F32)
        e = unit(p)[0].astype(BF)
        e_txt[rows, :] = e
        logits = scale * lax.dot_general(e, emb[...], NT, preferred_element_type=F32) + bias
        match = lax.broadcasted_iota(jnp.int32, logits.shape, 0) + s * SEG == pos
        sg = scale / (1.0 + jnp.exp(jnp.where(match, logits, -logits)))
        w = jnp.where(match, -sg, sg).astype(BF)
        wt[rows, :] = w
        g = jnp.dot(w, emb[...], preferred_element_type=F32)
        own1[s] = g[:32]
        s1[s] = g.astype(BF).reshape(4, 32, D)
        sends = []
        for d in (2, 1, 3):
            cp = remote(s1.at[s, d], r1.at[s, d], sem_1s.at[s, d], sem_1r.at[s, d], **along(half, -d, False))
            cp.start()
            sends.append(cp)
        return sends

    first = {0: segment(0, bulk0), 1: segment(1, bulk1)}
    first[3] = segment(3, bulk3)
    first[2] = segment(2, bulk2)

    def image_part(half):
        def step(i, carry):
            cols = pl.ds(pl.multiple_of(half * NI + i * 128, 128), 128)
            g = lax.dot_general(wt[:, cols], e_txt[...], TN, preferred_element_type=F32)
            rows = pl.ds(pl.multiple_of(i * 128, 128), 128)
            if half == 1:
                gimg_out[rows, :] = g.astype(BF)
            else:
                gimg[rows, :] = g
            return carry
        lax.fori_loop(0, 2, step, 0)

    image_part(1)
    core_grad = remote(gimg_out, gimg_in, sem_cs.at[2], sem_cr.at[2], dc=1)
    core_grad.start()

    def second(s):
        half = s % 2
        for cp in first[s]:
            cp.wait_recv()
        acc = own1[s] + r1[s, 1].astype(F32) + r1[s, 2].astype(F32) + r1[s, 3].astype(F32)
        own2[s] = acc[:8]
        s2[s] = acc.astype(BF).reshape(4, 8, D)
        sends = []
        for d in (2, 1, 3):
            cp = remote(s2.at[s, d], r2.at[s, d], sem_2s.at[s, d], sem_2r.at[s, d], **along(half, -d, True))
            cp.start()
            sends.append(cp)
        return sends

    def third(s, sends):
        for cp in sends:
            cp.wait_recv()
        acc = own2[s] + r2[s, 1].astype(F32) + r2[s, 2].astype(F32) + r2[s, 3].astype(F32)
        out = []
        for i in (3, 2, 1, 0):
            k = 4 * s + i
            row = acc[2 * i : 2 * i + 2, :]
            if k == 0:
                own3[...] = row
            else:
                zout[k] = row.astype(BF)
                cp = remote(zout.at[k], zr.at[k], sem_3s.at[k], sem_3r.at[k], dz=-STEPS[k])
                cp.start()
                out.append(cp)
        return out

    second0, second1 = second(0), second(1)
    image_part(0)
    second3, second2 = second(3), second(2)
    seconds = second0 + second1 + second2 + second3
    thirds = third(0, second0) + third(1, second1)
    thirds += third(3, second3) + third(2, second2)

    core_grad.wait()

    def finish(i, carry):
        rows = pl.ds(pl.multiple_of(i * 64, 64), 64)
        g = gimg[rows, :] + gimg_in[rows, :].astype(F32)
        u, r = unit(imgs[0, rows, :].astype(F32))
        g = (g - u * jnp.sum(u * g, axis=-1, keepdims=True)) * r
        gimg_out[rows, :] = g.astype(BF)
        return carry

    lax.fori_loop(0, NI // 64, finish, 0)
    store = pltpu.make_async_copy(gimg_out, out_img, sem_l.at[4])
    store.start()

    sent = list(zs.values()) + [on0, on1] + small0 + small1 + small2 + small3 + bulk0 + bulk1 + bulk2 + bulk3
    sent += first[0] + first[1] + first[2] + first[3] + seconds + thirds
    for cp in sent:
        cp.wait_send()
    store.wait()
    u, r = unit(proj_own[...])

    for cp in thirds:
        cp.wait_recv()
    total = own3[...]
    for k in range(1, 16):
        total = total + zr[k].astype(F32)
    pg = ((total - u * jnp.sum(u * total, axis=-1, keepdims=True)) * r).astype(BF)
    out_txt[...] = lax.dot_general(pg, wv[...], NT, preferred_element_type=F32)


def local(images, texts, text_proj, labels, logit_scale, logit_bias):
    vmem = pl.BlockSpec(memory_space=pltpu.VMEM)
    hbm = pl.BlockSpec(memory_space=pltpu.HBM)
    anywhere = pl.BlockSpec(memory_space=pl.ANY)
    dma = pltpu.SemaphoreType.DMA
    scratch = [
        pltpu.SMEM((2, 1, 1), F32),
        pltpu.VMEM((2, NI, D), BF),
        pltpu.VMEM((2 * NI, D), BF),
        pltpu.VMEM((D, D), BF),
        pltpu.VMEM((NI,), jnp.int32),
        pltpu.VMEM((NI,), jnp.int32),
        pltpu.VMEM((16, 2, D), BF),
        pltpu.VMEM((4, 4, 4, 8, D), BF),
        pltpu.VMEM((512, D), BF),
        pltpu.VMEM((512, 2 * NI), BF),
        pltpu.VMEM((2, D), F32),
        pltpu.VMEM((NI, D), BF),
        pltpu.VMEM((NI, D), BF),
        pltpu.VMEM((NI, D), F32),
        pltpu.VMEM((4, 32, D), F32),
        pltpu.VMEM((4, 4, 32, D), BF),
        pltpu.VMEM((4, 4, 32, D), BF),
        pltpu.VMEM((4, 8, D), F32),
        pltpu.VMEM((4, 4, 8, D), BF),
        pltpu.VMEM((4, 4, 8, D), BF),
        pltpu.VMEM((2, D), F32),
        pltpu.VMEM((16, 2, D), BF),
        pltpu.VMEM((16, 2, D), BF),
        dma((7,)), dma((3,)), dma((3,)), dma((16,)), dma((16,)),
        dma((4, 4)), dma((4, 4)), dma((4, 4)), dma((4, 4)),
        dma((4, 4)), dma((4, 4)), dma((4, 4)), dma((4, 4)), dma((16,)), dma((16,)),
    ]
    return pl.pallas_call(
        kernel,
        out_shape=(
            jax.ShapeDtypeStruct((NI, D), BF),
            jax.ShapeDtypeStruct((2, D), F32),
        ),
        in_specs=[hbm] * 6,
        out_specs=(anywhere, vmem),
        scratch_shapes=scratch,
        compiler_params=pltpu.CompilerParams(
            collective_id=0, has_side_effects=True, vmem_limit_bytes=40 * 2**20
        ),
        cost_estimate=pl.CostEstimate(flops=4 * 10**9, bytes_accessed=8 * 10**6, transcendentals=10**6),
        name="reward_backward",
    )(
        *[pltpu.with_memory_space_constraint(a, pltpu.HBM) for a in (images, texts, text_proj, labels)],
        logit_scale.reshape(1, 1),
        logit_bias.reshape(1, 1),
    )


def solution(mesh):
    in_specs = (P(("blk", "grp"), None), P(("blk", "grp"), None), P(), P(("blk", "grp")), P(), P())
    out_specs = (P(("blk", "grp"), None), P(("blk", "grp"), None))
    return jax.shard_map(local, mesh=mesh, in_specs=in_specs, out_specs=out_specs, check_vma=False)
```

time: 1160 us -> 57.7 us (0.05)
  the two profiles are of different devices: /device:TPU:6 before, /device:TPU:8 now
where the time goes in v2:
time: 57.7 us; the launch traced here: 57.6 us
  Pallas kernels  54.2 us (94%)
  between operations  1.93 us (3%)
  local copies, waits for them, and re-layouts  1.42 us (2%)
    pallas_call x1, Pallas kernels, local(): pl.pallas_call(kernel, out_shape=(jax.ShapeDtypeStruct((NI, D), BF), jax....  54.2 us
    unnamed x2, local copies, waits for them, and re-layouts  1.42 us

profile of v2, /device:TPU:8, one launch (start us, length us, event | category | flops | bytes accessed | tf_op | source)
XLA Modules:
  0.0 57.6 jit_solution(5713692361150288059)
XLA Ops:
  1.9 54.2 %reward_backward.1 = (bf16[256,1152]{1,0:T(8,128)(2,1)S(1)}, f32[2,1152]{1,0:T(2,128)S(1)}) custom-call(bf16[256,1152]{1,0:T(8,128)(2,1)} %images.1, bf16[2,1152]{1,0:T(2,128)(2,1)} %texts.1, bf16[1152,1152]{1,0:T(8,128)(2,1)} %proj_w.1, s32[256]{0:T(256)} %labels.1, f32[1,1]{1,0:T(1,128)} %bitcast.2.scale_ref, f32[1,1]{1,0:T(1,128)} %bitcast.3.bias_ref), custom_call_target="tpu_custom_call" | custom-call | flops 4000000000 | bytes 8000000 | tf_op jit(solution)/shard_map/reward_backward/pallas_call | solution.py:303
  56.2 0.8 %copy.12 = bf16[256,1152]{1,0:T(8,128)(2,1)} copy(bf16[256,1152]{1,0:T(8,128)(2,1)S(1)} %get-tuple-element.4) | data formatting | bytes 1179648
  57.0 0.6 %copy.13 = f32[2,1152]{1,0:T(2,128)} copy(f32[2,1152]{1,0:T(2,128)S(1)} %get-tuple-element.5) | data formatting | bytes 18432

commit v3 on v2

v3 whole, which is shorter than its diff:
```python
import jax
import jax.numpy as jnp
from jax import lax
from jax.experimental import pallas as pl
from jax.experimental.pallas import tpu as pltpu
from jax.sharding import PartitionSpec as P

MESH = pl.DeviceIdType.MESH
BF = jnp.bfloat16
F32 = jnp.float32
D = 1152
NI = 256
EPS = 1e-06
NT = (((1,), (1,)), ((), ()))
TN = (((0,), (0,)), ((), ()))
STEPS = (0, -1, -2, -3, 1, 2, 3, 4, 5, 6, 7, 8, -4, -5, -6, -7)
NEAR = (7, 6, 3, 5, 2, 4, 1)
SEG = 128
COLS = (slice(0, 640), slice(640, D))
WIDE = (640, 512)
ROWS = {0: 0, 1: SEG, 3: 2 * SEG, 2: 3 * SEG, 4: 4 * SEG}
LESS, MORE = 3 * SEG, 5 * SEG


def mod(a, n):
    return lax.rem(a + n, n)


def unit(v):
    r = lax.rsqrt(jnp.sum(v * v, axis=-1, keepdims=True) + EPS)
    return v * r, r


def kernel(
    images, texts, proj_w, labels, scale_ref, bias_ref,
    out_img, out_txt,
    scal, imgs, emb, wv, wvt, lab_a, lab_b, zin, txa, txb, e_txt, wt, proj_own, gimg_out, gimg_in, gimg,
    own1a, own1b, s1a, s1b, r1a, r1b, own2a, own2b, s2a, s2b, r2a, r2b, own3, zout, zr,
    sem_l, sem_cs, sem_cr, sem_zs, sem_zr, sem_os, sem_or, sem_ss, sem_sr, sem_bs, sem_br,
    sem_1s, sem_1r, sem_2s, sem_2r, sem_3s, sem_3r,
):
    blk = lax.axis_index("blk")
    grp = lax.axis_index("grp")
    c = lax.rem(blk, 2)
    z = lax.rem(grp, 4) * 4 + lax.div(blk, 2)
    x = lax.div(grp, 16)
    y = lax.rem(lax.div(grp, 4), 4)
    wide = pl.when(c == 1)
    narrow = pl.when(c == 0)
    tx, own1, s1, r1 = (txa, txb), (own1a, own1b), (s1a, s1b), (r1a, r1b)
    own2, s2, r2 = (own2a, own2b), (s2a, s2b), (r2a, r2b)
    parts = (0, 1)

    def device(core, dx=0, dy=0, dz=0):
        tz = mod(z + dz, 16)
        return {
            "blk": lax.rem(tz, 4) * 2 + core,
            "grp": mod(x + dx, 4) * 16 + mod(y + dy, 4) * 4 + lax.div(tz, 4),
        }

    def remote(src, dst, ss, rs, core, **to):
        return pltpu.make_async_remote_copy(
            src_ref=src, dst_ref=dst, send_sem=ss, recv_sem=rs,
            device_id=device(core, **to), device_id_type=MESH,
        )

    def along(p, by, first):
        return {"dx" if (p == 0) == first else "dy": by}

    def z_copy(k):
        return remote(zin.at[0], zin.at[k], sem_zs.at[k], sem_zr.at[k], c, dz=STEPS[k])

    def on_copy(s, p):
        to = 3 if s == 0 else 4 - 2 * c
        return remote(
            tx[p].at[s, 0, 0], tx[p].at[to, 0, 0], sem_os.at[s, p], sem_or.at[to, p], c if s == 0 else 1, dz=(-4, 4)[s]
        )

    def on_arrival(s, p):
        return remote(tx[p].at[0, 0, 0], tx[p].at[s, 0, 0], sem_os.at[0, p], sem_or.at[s, p], c, dz=4)

    def small_copy(s, p, d):
        t = tx[p]
        return remote(t.at[s, 0, 0], t.at[s, 0, d], sem_ss.at[s, p, d], sem_sr.at[s, p, d], c, **along(p, d, True))

    def bulk_copy(s, p, d):
        t = tx[p]
        return remote(t.at[s, 0], t.at[s, d], sem_bs.at[s, p, d], sem_br.at[s, p, d], c, **along(p, d, False))

    def first_copy(s, p, d):
        return remote(s1[p].at[s, d], r1[p].at[s, d], sem_1s.at[s, p, d], sem_1r.at[s, p, d], c, **along(p, -d, False))

    def second_copy(s, p, d):
        return remote(s2[p].at[s, d], r2[p].at[s, d], sem_2s.at[s, p, d], sem_2r.at[s, p, d], c, **along(p, -d, True))

    def third_copy(k):
        return remote(zout.at[k], zr.at[k], sem_3s.at[k], sem_3r.at[k], c, dz=-STEPS[k])

    def third_extra(k):
        return remote(zout.at[k + 8], zr.at[k], sem_3s.at[k + 8], sem_3r.at[k], 0, dz=-STEPS[k])

    fan = [(d, p) for d in (2, 1, 3) for p in parts]

    load_txt = pltpu.make_async_copy(texts, zin.at[0], sem_l.at[0])
    load_lab = pltpu.make_async_copy(labels, lab_a, sem_l.at[1])
    load_img = pltpu.make_async_copy(images, imgs.at[0], sem_l.at[2])
    rest = [
        pltpu.make_async_copy(proj_w, wv, sem_l.at[3]),
        pltpu.make_async_copy(scale_ref, scal.at[0], sem_l.at[5]),
        pltpu.make_async_copy(bias_ref, scal.at[1], sem_l.at[6]),
    ]
    for cp in [load_txt, load_lab, load_img] + rest:
        cp.start()

    barrier = pltpu.get_barrier_semaphore()
    chips = [dict(dz=d) for d in (4, -4, 3, -3, 2, -2, 1, -1)]
    chips += [dict(dx=d) for d in (1, 2, 3)] + [dict(dy=d) for d in (1, 2, 3)]
    for p in chips:
        pl.semaphore_signal(barrier, inc=1, device_id=device(c, **p), device_id_type=MESH)
    pl.semaphore_signal(barrier, inc=1, device_id=device(1 - c), device_id_type=MESH)

    @wide
    def _():
        pl.semaphore_signal(barrier, inc=1, device_id=device(0, dz=-4), device_id_type=MESH)

    load_txt.wait()

    @narrow
    def _():
        pl.semaphore_wait(barrier, len(chips) + 2)

    @wide
    def _():
        pl.semaphore_wait(barrier, len(chips) + 1)

    for k in NEAR:
        z_copy(k).start()

    load_lab.wait()
    load_img.wait()
    core_lab = remote(lab_a, lab_b, sem_cs.at[0], sem_cr.at[0], 1 - c)
    core_img = remote(imgs.at[0], imgs.at[1], sem_cs.at[1], sem_cr.at[1], 1 - c)
    core_lab.start()
    core_img.start()

    def embed(half):
        def step(i, carry):
            u, _ = unit(imgs[half, pl.ds(pl.multiple_of(i * 64, 64), 64), :].astype(F32))
            emb[pl.ds(pl.multiple_of(half * NI + i * 64, 64), 64), :] = u.astype(BF)
            return carry
        lax.fori_loop(0, NI // 64, step, 0)

    embed(0)

    def place(s):
        for k in range(4 * s, 4 * s + 4):
            if k:
                z_copy(k).wait_recv()
        rows = zin[4 * s : 4 * s + 4].astype(F32).reshape(8, D).astype(BF)
        for p in parts:
            tx[p][s, 0, 0] = rows[:, COLS[p]]
            on_copy(s, p).start()

    def small(s):
        for d, p in fan:
            small_copy(s, p, d).start()

    def arrive(s):
        for p in parts:
            on_arrival(s, p).wait_recv()
        small(s)

    def spread(s):
        for d, p in fan:
            small_copy(s, p, d).wait_recv()
        for d, p in fan:
            bulk_copy(s, p, d).start()

    for s in (0, 1):
        place(s)
        small(s)
    spread(0)
    spread(1)
    core_lab.wait()
    core_img.wait()
    embed(1)
    for cp in rest:
        cp.wait()
    proj_own[...] = jnp.dot(zin[0], wv[...], preferred_element_type=F32)
    wvt[...] = wv[...].T
    arrive(3)

    @wide
    def _():
        arrive(2)
        arrive(4)

    spread(3)

    @wide
    def _():
        spread(2)
        spread(4)

    scale = scal[0, 0, 0]
    bias = scal[1, 0, 0]

    lab = jnp.concatenate([lab_a[...][None, :], lab_b[...][None, :]], axis=1)
    ez = mod(z - (((lab >> 1) & 3) * 4 + ((lab >> 8) & 3)), 16)
    ey = mod(y - ((lab >> 3) & 3), 4)
    ex = mod(x - ((lab >> 5) & 3), 4)
    kz = jnp.where(ez == 0, 0, jnp.where(ez <= 8, ez + 3, jnp.where(ez >= 13, 16 - ez, 24 - ez)))
    seg = kz >> 2
    base = jnp.where(seg == 3, ROWS[3], jnp.where(seg == 2, ROWS[2], seg * SEG))
    within = ey * 32 + ex * 8 + (kz & 3) * 2 + (lab & 1)
    owner = (lab >> 7) & 1
    pos = jnp.where((seg == 2) & (c == 0), -1, base + within)
    pos = jnp.where(owner == c, pos, jnp.where((seg == 2) & (c == 1), ROWS[4] + within, -1))

    def segment(s):
        for d, p in fan:
            bulk_copy(s, p, d).wait_recv()
        rows = pl.ds(ROWS[s], SEG)
        ta = txa[s].reshape(SEG, WIDE[0])
        tb = jnp.concatenate([txb[s, j, i] for i in range(4) for j in range(4)], axis=0)
        p = jnp.dot(ta, wv[COLS[0], :], preferred_element_type=F32)
        p = p + jnp.dot(tb, wv[COLS[1], :], preferred_element_type=F32)
        e = unit(p)[0].astype(BF)
        e_txt[rows, :] = e
        logits = scale * lax.dot_general(e, emb[...], NT, preferred_element_type=F32) + bias
        match = lax.broadcasted_iota(jnp.int32, logits.shape, 0) + ROWS[s] == pos
        sg = scale / (1.0 + jnp.exp(jnp.where(match, logits, -logits)))
        w = jnp.where(match, -sg, sg).astype(BF)
        wt[rows, :] = w
        g = jnp.dot(w, emb[...], preferred_element_type=F32)
        own1a[s] = g[:32, COLS[0]]
        s1a[s] = g[:, COLS[0]].astype(BF).reshape(4, 32, WIDE[0])
        for i in range(4):
            for j in range(4):
                b = g[i * 32 + j * 8 : i * 32 + j * 8 + 8, COLS[1]]
                if j == 0:
                    own1b[s, i] = b
                else:
                    s1b[s, j, i] = b.astype(BF)
        for d, p in fan:
            first_copy(s, p, d).start()

    for s in (0, 1, 3):
        segment(s)

    @wide
    def _():
        segment(2)
        segment(4)

    def image_part(half):
        def over(n):
            def step(i, carry):
                cols = pl.ds(pl.multiple_of(half * NI + i * 128, 128), 128)
                g = lax.dot_general(wt[:n, cols], e_txt[:n, :], TN, preferred_element_type=F32)
                rows = pl.ds(pl.multiple_of(i * 128, 128), 128)
                if half == 1:
                    gimg_out[rows, :] = g.astype(BF)
                else:
                    gimg[rows, :] = g
                return carry
            lax.fori_loop(0, 2, step, 0)

        @narrow
        def _():
            over(LESS)

        @wide
        def _():
            over(MORE)

    image_part(1)
    core_grad = remote(gimg_out, gimg_in, sem_cs.at[2], sem_cr.at[2], 1 - c)
    core_grad.start()

    def second(s):
        for p in parts:
            shape = (4, 8, WIDE[p])
            acc = own1[p][s].reshape(shape)
            for d in (1, 2, 3):
                first_copy(s, p, d).wait_recv()
                acc = acc + r1[p][s, d].astype(F32).reshape(shape)
            own2[p][s] = acc[0]
            s2[p][s] = acc.astype(BF)
            for d in (2, 1, 3):
                second_copy(s, p, d).start()

    def third(s):
        sums = []
        for p in parts:
            acc = own2[p][s]
            for d in (1, 2, 3):
                second_copy(s, p, d).wait_recv()
                acc = acc + r2[p][s, d].astype(F32)
            sums.append(acc)
        acc = jnp.concatenate(sums, axis=1)
        for i in (3, 2, 1, 0):
            row = acc[2 * i : 2 * i + 2, :]
            if s == 4:
                zout[16 + i] = row.astype(BF)
                third_extra(8 + i).start()
            elif s == i == 0:
                own3[...] = row
            else:
                zout[4 * s + i] = row.astype(BF)
                third_copy(4 * s + i).start()

    second(0)
    second(1)
    image_part(0)
    second(3)

    @wide
    def _():
        second(2)
        second(4)

    third(0)
    third(1)
    third(3)

    @wide
    def _():
        third(2)
        third(4)

    core_grad.wait()

    def finish(i, carry):
        rows = pl.ds(pl.multiple_of(i * 64, 64), 64)
        g = gimg[rows, :] + gimg_in[rows, :].astype(F32)
        u, r = unit(imgs[0, rows, :].astype(F32))
        g = (g - u * jnp.sum(u * g, axis=-1, keepdims=True)) * r
        gimg_out[rows, :] = g.astype(BF)
        return carry

    lax.fori_loop(0, NI // 64, finish, 0)
    store = pltpu.make_async_copy(gimg_out, out_img, sem_l.at[4])
    store.start()

    def left(s):
        for d, p in fan:
            small_copy(s, p, d).wait_send()
            bulk_copy(s, p, d).wait_send()
            first_copy(s, p, d).wait_send()
            second_copy(s, p, d).wait_send()

    for k in NEAR:
        z_copy(k).wait_send()
    for s in (0, 1):
        for p in parts:
            on_copy(s, p).wait_send()
    for s in (0, 1, 3):
        left(s)
    for k in (1, 2, 3, 4, 5, 6, 7, 12, 13, 14, 15):
        third_copy(k).wait_send()

    @wide
    def _():
        left(2)
        left(4)
        for k in (8, 9, 10, 11):
            third_copy(k).wait_send()
            third_extra(k).wait_send()

    store.wait()
    u, r = unit(proj_own[...])
    for k in range(1, 16):
        third_copy(k).wait_recv()
    total = own3[...]
    for k in range(1, 16):
        total = total + zr[k].astype(F32)
    pg = ((total - u * jnp.sum(u * total, axis=-1, keepdims=True)) * r).astype(BF)
    out_txt[...] = jnp.dot(pg, wvt[...], preferred_element_type=F32)


def local(images, texts, text_proj, labels, logit_scale, logit_bias):
    vmem = pl.BlockSpec(memory_space=pltpu.VMEM)
    hbm = pl.BlockSpec(memory_space=pltpu.HBM)
    anywhere = pl.BlockSpec(memory_space=pl.ANY)
    dma = pltpu.SemaphoreType.DMA
    scratch = [
        pltpu.SMEM((2, 1, 1), F32),
        pltpu.VMEM((2, NI, D), BF),
        pltpu.VMEM((2 * NI, D), BF),
        pltpu.VMEM((D, D), BF),
        pltpu.VMEM((D, D), BF),
        pltpu.VMEM((NI,), jnp.int32),
        pltpu.VMEM((NI,), jnp.int32),
        pltpu.VMEM((8, 2, D), BF),
        *[pltpu.VMEM((5, 4, 4, 8, w), BF) for w in WIDE],
        pltpu.VMEM((MORE, D), BF),
        pltpu.VMEM((MORE, 2 * NI), BF),
        pltpu.VMEM((2, D), F32),
        pltpu.VMEM((NI, D), BF),
        pltpu.VMEM((NI, D), BF),
        pltpu.VMEM((NI, D), F32),
        pltpu.VMEM((5, 32, WIDE[0]), F32),
        pltpu.VMEM((5, 4, 8, WIDE[1]), F32),
        pltpu.VMEM((5, 4, 32, WIDE[0]), BF),
        pltpu.VMEM((5, 4, 4, 8, WIDE[1]), BF),
        pltpu.VMEM((5, 4, 32, WIDE[0]), BF),
        pltpu.VMEM((5, 4, 4, 8, WIDE[1]), BF),
        *[pltpu.VMEM((5, 8, w), F32) for w in WIDE],
        *[pltpu.VMEM((5, 4, 8, w), BF) for w in WIDE],
        *[pltpu.VMEM((5, 4, 8, w), BF) for w in WIDE],
        pltpu.VMEM((2, D), F32),
        pltpu.VMEM((20, 2, D), BF),
        pltpu.VMEM((16, 2, D), BF),
        dma((7,)), dma((3,)), dma((3,)),
        dma((8,)), dma((8,)), dma((2, 2)), dma((5, 2)),
        *[dma((5, 2, 4)) for _ in range(8)], dma((20,)), dma((16,)),
    ]
    return pl.pallas_call(
        kernel,
        out_shape=(
            jax.ShapeDtypeStruct((NI, D), BF),
            jax.ShapeDtypeStruct((2, D), F32),
        ),
        in_specs=[hbm] * 6,
        out_specs=(anywhere, vmem),
        scratch_shapes=scratch,
        compiler_params=pltpu.CompilerParams(
            collective_id=0, has_side_effects=True, vmem_limit_bytes=40 * 2**20
        ),
        cost_estimate=pl.CostEstimate(flops=4 * 10**9, bytes_accessed=8 * 10**6, transcendentals=10**6),
        name="reward_backward",
    )(
        *[pltpu.with_memory_space_constraint(a, pltpu.HBM) for a in (images, texts, text_proj, labels)],
        logit_scale.reshape(1, 1),
        logit_bias.reshape(1, 1),
    )


def solution(mesh):
    in_specs = (P(("blk", "grp"), None), P(("blk", "grp"), None), P(), P(("blk", "grp")), P(), P())
    out_specs = (P(("blk", "grp"), None), P(("blk", "grp"), None))
    return jax.shard_map(local, mesh=mesh, in_specs=in_specs, out_specs=out_specs, check_vma=False)
```

time: 57.7 us -> 55.6 us (0.964)
  the two profiles are of different devices: /device:TPU:8 before, /device:TPU:6 now
where the time goes in v3:
time: 55.6 us; the launch traced here: 55.1 us
  Pallas kernels  51.7 us (93%)
  between operations  1.93 us (3%)
  local copies, waits for them, and re-layouts  1.42 us (3%)
    pallas_call x1, Pallas kernels, local(): pl.pallas_call(kernel, out_shape=(jax.ShapeDtypeStruct((NI, D), BF), jax....  51.7 us
    unnamed x2, local copies, waits for them, and re-layouts  1.42 us

profile of v3, /device:TPU:6, one launch (start us, length us, event | category | flops | bytes accessed | tf_op | source)
XLA Modules:
  0.0 55.1 jit_solution(12352788432436490585)
XLA Ops:
  1.9 51.7 %reward_backward.1 = (bf16[256,1152]{1,0:T(8,128)(2,1)S(1)}, f32[2,1152]{1,0:T(2,128)S(1)}) custom-call(bf16[256,1152]{1,0:T(8,128)(2,1)} %images.1, bf16[2,1152]{1,0:T(2,128)(2,1)} %texts.1, bf16[1152,1152]{1,0:T(8,128)(2,1)} %proj_w.1, s32[256]{0:T(256)} %labels.1, f32[1,1]{1,0:T(1,128)} %bitcast.2.scale_ref, f32[1,1]{1,0:T(1,128)} %bitcast.3.bias_ref), custom_call_target="tpu_custom_call" | custom-call | flops 4000000000 | bytes 8000000 | tf_op jit(solution)/shard_map/reward_backward/pallas_call | solution.py:419
  53.6 0.8 %copy.12 = bf16[256,1152]{1,0:T(8,128)(2,1)} copy(bf16[256,1152]{1,0:T(8,128)(2,1)S(1)} %get-tuple-element.4) | data formatting | bytes 1179648
  54.5 0.6 %copy.13 = f32[2,1152]{1,0:T(2,128)} copy(f32[2,1152]{1,0:T(2,128)S(1)} %get-tuple-element.5) | data formatting | bytes 18432

commit v4 on v3

--- a/solution.py
+++ b/solution.py
@@ -184,17 +184,17 @@
     core_lab.wait()
     core_img.wait()
     embed(1)
+    arrive(3)
+
+    @wide
+    def _():
+        arrive(2)
+        arrive(4)
+
     for cp in rest:
         cp.wait()
     proj_own[...] = jnp.dot(zin[0], wv[...], preferred_element_type=F32)
     wvt[...] = wv[...].T
-    arrive(3)
-
-    @wide
-    def _():
-        arrive(2)
-        arrive(4)
-
     spread(3)
 
     @wide
@@ -370,10 +370,9 @@
 
     store.wait()
     u, r = unit(proj_own[...])
+    total = own3[...]
     for k in range(1, 16):
         third_copy(k).wait_recv()
-    total = own3[...]
-    for k in range(1, 16):
         total = total + zr[k].astype(F32)
     pg = ((total - u * jnp.sum(u * total, axis=-1, keepdims=True)) * r).astype(BF)
     out_txt[...] = jnp.dot(pg, wvt[...], preferred_element_type=F32)

time: 55.6 us -> 55.8 us (level)
  no operation moved by 1% of the time
where the time goes in v4:
time: 55.8 us; the launch traced here: 55.1 us
  Pallas kernels  51.7 us (93%)
  between operations  1.93 us (3%)
  local copies, waits for them, and re-layouts  1.42 us (3%)
    pallas_call x1, Pallas kernels, local(): pl.pallas_call(kernel, out_shape=(jax.ShapeDtypeStruct((NI, D), BF), jax....  51.7 us
    unnamed x2, local copies, waits for them, and re-layouts  1.42 us

profile of v4, /device:TPU:6, one launch (start us, length us, event | category | flops | bytes accessed | tf_op | source)
XLA Modules:
  0.0 55.1 jit_solution(3743399674754983569)
XLA Ops:
  1.9 51.7 %reward_backward.1 = (bf16[256,1152]{1,0:T(8,128)(2,1)S(1)}, f32[2,1152]{1,0:T(2,128)S(1)}) custom-call(bf16[256,1152]{1,0:T(8,128)(2,1)} %images.1, bf16[2,1152]{1,0:T(2,128)(2,1)} %texts.1, bf16[1152,1152]{1,0:T(8,128)(2,1)} %proj_w.1, s32[256]{0:T(256)} %labels.1, f32[1,1]{1,0:T(1,128)} %bitcast.2.scale_ref, f32[1,1]{1,0:T(1,128)} %bitcast.3.bias_ref), custom_call_target="tpu_custom_call" | custom-call | flops 4000000000 | bytes 8000000 | tf_op jit(solution)/shard_map/reward_backward/pallas_call | solution.py:418
  53.6 0.8 %copy.12 = bf16[256,1152]{1,0:T(8,128)(2,1)} copy(bf16[256,1152]{1,0:T(8,128)(2,1)S(1)} %get-tuple-element.4) | data formatting | bytes 1179648
  54.5 0.6 %copy.13 = f32[2,1152]{1,0:T(2,128)} copy(f32[2,1152]{1,0:T(2,128)S(1)} %get-tuple-element.5) | data formatting | bytes 18432
